TPU v7x, 32 devices: a whole 2x2x4 slice. The times are simulated.
32 devices in a mesh: dom: 4 (over x, core), ctx: 8 (over z, y).
Axes of the slice: x: 2, y: 2, z: 4, core: 2. Of those that a mesh axis runs over, the one named last changes fastest.
Arguments:
- prompt_kv: bfloat16 [16384, 1024], P('ctx'), may hold values from -6 to 6
- suffix_kv: bfloat16 [32, 12, 1024], P('dom'), may hold values from -12 to 12
- new_kv: bfloat16 [4, 32, 1024], P(None, 'dom'), may hold values from -12 to 12
- queries: bfloat16 [4, 32, 4096], P(None, 'dom', 'ctx'), may hold values from -128 to 128
- ancestors: int32 [4, 32], P(None, 'dom'), may hold values from 0 to 31, as said below
Outputs:
- attended: float32 [4, 32, 4096], P(None, 'dom', 'ctx')
- suffix_out: bfloat16 [32, 16, 1024], P('dom')
Inputs may be any that keep to these rules, and one draw needn't show every extreme that they name: ancestors[s, p] differs from p by at most 4, and by exactly 4 for some particle of every step.
All inputs are finite; a program needn't handle non-finite values.
Results may differ from a plain program's by a relative error of at most 0.0049.
Values may be sent and summed in bfloat16 or wider, within the bound.
A program may use at most 128 MiB of HBM per device.

v0:
```python
import jax
import jax.numpy as jnp
from jax import lax
from jax.sharding import PartitionSpec as P

HEADS = 32
HEAD_DIM = 128


floor_score = -1e30


def joined(array, axis, combine):
    everything = jax.tree.map(lambda part: lax.all_gather(part, axis), array)
    initial = jax.tree.map(lambda part: part[0], everything)

    def hop(k, so_far):
        return combine(so_far, jax.tree.map(lambda part: part[k], everything))

    return lax.fori_loop(1, lax.axis_size(axis), hop, initial)


def extended_2(cells, sides, width):
    for axis, dim in sides:
        count = lax.axis_size(axis)
        ends = count - 1
        head = lax.slice_in_dim(cells, 0, width, axis=dim)
        tail = lax.slice_in_dim(cells, cells.shape[dim] - width, cells.shape[dim], axis=dim)
        cells = jnp.concatenate(
            [
                lax.ppermute(tail, axis, [(i, (i + 1) % count) for i in range(ends)]),
                cells,
                lax.ppermute(head, axis, [((i + 1) % count, i) for i in range(ends)]),
            ],
            axis=dim,
        )
    return cells


def merge_softmax(first, second):
    first_peak, first_total, first_sum = first
    second_peak, second_total, second_sum = second
    highest = jnp.maximum(first_peak, second_peak)
    first_factor = jnp.exp(first_peak - highest)
    second_factor = jnp.exp(second_peak - highest)
    total = first_total * first_factor + second_total * second_factor
    summed = first_sum * first_factor[..., None] + second_sum * second_factor[..., None]
    return (highest, total, summed)


def shards(prompt_kv, suffix_kv, new_kv, queries, ancestors):
    part_rows = suffix_kv.shape[0]
    history = suffix_kv.shape[1]
    row_width = suffix_kv.shape[2]
    step_count = queries.shape[0]
    head_size = HEAD_DIM
    key_heads = row_width // (2 * head_size)
    key_width = key_heads * head_size
    head_count = HEADS
    group_size = head_count // key_heads
    ctx_count = lax.axis_size("ctx")
    own_heads = head_count // ctx_count
    column = lax.axis_index("ctx")
    reach = part_rows // 2
    slots = history + step_count
    inverse_root = 1.0 / head_size**0.5
    prompt_keys = prompt_kv[:, :key_width].reshape(-1, key_heads, head_size)
    prompt_vals = prompt_kv[:, key_width:].reshape(-1, key_heads, head_size)
    cache = jnp.concatenate(
        [suffix_kv, jnp.zeros((part_rows, step_count, row_width), jnp.bfloat16)], axis=1
    )
    first_row = lax.axis_index("dom") * part_rows - reach
    extended = jnp.arange(part_rows + 2 * reach, dtype=jnp.int32)
    every_query = lax.all_gather(queries, "ctx", axis=2, tiled=True)
    results = []
    for moment in range(step_count):
        cache = cache.at[:, history + moment, :].set(new_kv[moment])
        query_now = every_query[moment]
        query_heads = query_now.reshape(part_rows, key_heads, group_size, head_size)
        prompt_score = (
            jnp.einsum(
                "pged,tgd->pget", query_heads, prompt_keys, preferred_element_type=jnp.float32
            )
            * inverse_root
        )
        prompt_peak = prompt_score.max(-1)
        prompt_weight = jnp.exp(prompt_score - prompt_peak[..., None])
        prompt_total = prompt_weight.sum(-1)
        prompt_sum = jnp.einsum(
            "pget,tgd->pged",
            prompt_weight.astype(jnp.bfloat16),
            prompt_vals,
            preferred_element_type=jnp.float32,
        )
        suffix_keys = cache[:, :, :key_width].reshape(part_rows, slots, key_heads, head_size)
        suffix_vals = cache[:, :, key_width:].reshape(part_rows, slots, key_heads, head_size)
        suffix_score = (
            jnp.einsum(
                "pged,psgd->pges", query_heads, suffix_keys, preferred_element_type=jnp.float32
            )
            * inverse_root
        )
        valid = jnp.arange(slots) <= history + moment
        suffix_score = jnp.where(valid, suffix_score, floor_score)
        suffix_peak = suffix_score.max(-1)
        suffix_weight = jnp.exp(suffix_score - suffix_peak[..., None])
        suffix_total = suffix_weight.sum(-1)
        suffix_sum = jnp.einsum(
            "pges,psgd->pged",
            suffix_weight.astype(jnp.bfloat16),
            suffix_vals,
            preferred_element_type=jnp.float32,
        )
        whole_peak, whole_total, whole_sum = joined(
            (prompt_peak, prompt_total, prompt_sum), "ctx", merge_softmax
        )
        mine_peak = lax.dynamic_slice_in_dim(
            whole_peak.reshape(part_rows, head_count), column * own_heads, own_heads, 1
        )
        mine_total = lax.dynamic_slice_in_dim(
            whole_total.reshape(part_rows, head_count), column * own_heads, own_heads, 1
        )
        mine_sum = lax.dynamic_slice_in_dim(
            whole_sum.reshape(part_rows, head_count, head_size), column * own_heads, own_heads, 1
        )
        own_peak = lax.dynamic_slice_in_dim(
            suffix_peak.reshape(part_rows, head_count), column * own_heads, own_heads, 1
        )
        own_total = lax.dynamic_slice_in_dim(
            suffix_total.reshape(part_rows, head_count), column * own_heads, own_heads, 1
        )
        own_sum = lax.dynamic_slice_in_dim(
            suffix_sum.reshape(part_rows, head_count, head_size), column * own_heads, own_heads, 1
        )
        highest = jnp.maximum(mine_peak, own_peak)
        prompt_factor = jnp.exp(mine_peak - highest)
        suffix_factor = jnp.exp(own_peak - highest)
        denominator = mine_total * prompt_factor + own_total * suffix_factor
        numerator = mine_sum * prompt_factor[..., None] + own_sum * suffix_factor[..., None]
        results.append(
            (numerator / denominator[..., None]).reshape(part_rows, own_heads * head_size)
        )
        local_parent = ancestors[moment] - first_row
        selector = (local_parent[:, None] == extended[None, :]).astype(jnp.bfloat16)
        widened = extended_2(cache, (("dom", 0),), reach)
        cache = jnp.einsum(
            "pq,qsw->psw", selector, widened, preferred_element_type=jnp.float32
        ).astype(jnp.bfloat16)
    return (jnp.stack(results), cache)


def solution(mesh):
    return jax.shard_map(
        shards,
        mesh=mesh,
        in_specs=(
            P("ctx", None),
            P("dom", None, None),
            P(None, "dom", None),
            P(None, "dom", "ctx"),
            P(None, "dom"),
        ),
        out_specs=(P(None, "dom", "ctx"), P("dom", None, None)),
        check_vma=False,
    )
```

profile of v0, /device:TPU:0, one launch (start us, length us, event | category | flops | bytes accessed | tf_op | source)
XLA Modules:
  0.0 400.5 jit_solution(1519209674463751309)
XLA Ops:
  7.2 32.7 %all_gather.75 = bf16[4,8,4096]{2,1,0:T(8,128)(2,1)S(1)} all-gather(bf16[4,8,512]{2,1,0:T(8,128)(2,1)} %param.24), channel_id=1, replica_groups=mesh['dom'=4,'ctx'=8] {'ctx'}, dimensions={2}, use_global_device_ids=true | all-gather | bytes 294912 | tf_op jit(solution)/shard_map/all_gather | solution.py:74
  40.0 3.8 fusion.140
  43.8 2.5 copy.140
  46.3 2.9 copy.141
  49.3 2.1 fusion.153
  59.5 2.1 fusion.149
  67.4 2.1 fusion.147
  72.5 2.2 fusion.21
  75.1 2.2 fusion.25
  77.8 31.1 %all-gather.1 = f32[64,4,8]{2,1,0:T(4,128)S(1)} all-gather(f32[8,4,8]{2,1,0:T(4,128)S(1)} %copy.71), channel_id=3, replica_groups=mesh['dom'=4,'ctx'=8] {'ctx'}, dimensions={0}, use_global_device_ids=true | all-gather | bytes 9216 | tf_op jit(solution)/shard_map/all_gather | solution.py:14
  108.8 30.7 %all-gather = f32[64,4,8]{2,1,0:T(4,128)S(1)} all-gather(f32[8,4,8]{2,1,0:T(4,128)S(1)} %copy.70), channel_id=2, replica_groups=mesh['dom'=4,'ctx'=8] {'ctx'}, dimensions={0}, use_global_device_ids=true | all-gather | bytes 9216 | tf_op jit(solution)/shard_map/all_gather | solution.py:14
  140.3 30.9 %all-gather.4 = f32[64,4,8]{2,1,0:T(4,128)S(1)} all-gather(f32[8,4,8]{2,1,0:T(4,128)S(1)} %copy.83), channel_id=6, replica_groups=mesh['dom'=4,'ctx'=8] {'ctx'}, dimensions={0}, use_global_device_ids=true | all-gather | bytes 9216 | tf_op jit(solution)/shard_map/all_gather | solution.py:14
  171.3 30.6 %all-gather.3 = f32[64,4,8]{2,1,0:T(4,128)S(1)} all-gather(f32[8,4,8]{2,1,0:T(4,128)S(1)} %copy.82), channel_id=5, replica_groups=mesh['dom'=4,'ctx'=8] {'ctx'}, dimensions={0}, use_global_device_ids=true | all-gather | bytes 9216 | tf_op jit(solution)/shard_map/all_gather | solution.py:14
  201.9 30.8 %all-gather.7 = f32[64,4,8]{2,1,0:T(4,128)S(1)} all-gather(f32[8,4,8]{2,1,0:T(4,128)S(1)} %copy.92), channel_id=9, replica_groups=mesh['dom'=4,'ctx'=8] {'ctx'}, dimensions={0}, use_global_device_ids=true | all-gather | bytes 9216 | tf_op jit(solution)/shard_map/all_gather | solution.py:14
  232.7 30.5 %all-gather.6 = f32[64,4,8]{2,1,0:T(4,128)S(1)} all-gather(f32[8,4,8]{2,1,0:T(4,128)S(1)} %copy.91), channel_id=8, replica_groups=mesh['dom'=4,'ctx'=8] {'ctx'}, dimensions={0}, use_global_device_ids=true | all-gather | bytes 9216 | tf_op jit(solution)/shard_map/all_gather | solution.py:14
  263.2 30.5 %all-gather.10 = f32[64,4,8]{2,1,0:T(4,128)S(1)} all-gather(f32[8,4,8]{2,1,0:T(4,128)S(1)} %copy.101), channel_id=12, replica_groups=mesh['dom'=4,'ctx'=8] {'ctx'}, dimensions={0}, use_global_device_ids=true | all-gather | bytes 9216 | tf_op jit(solution)/shard_map/all_gather | solution.py:14
  293.7 30.5 %all-gather.9 = f32[64,4,8]{2,1,0:T(4,128)S(1)} all-gather(f32[8,4,8]{2,1,0:T(4,128)S(1)} %copy.100), channel_id=11, replica_groups=mesh['dom'=4,'ctx'=8] {'ctx'}, dimensions={0}, use_global_device_ids=true | all-gather | bytes 9216 | tf_op jit(solution)/shard_map/all_gather | solution.py:14
  329.4 6.1 %collective-permute-done.3 = bf16[4,16,1024]{2,0,1:T(4,128)(2,1)S(1)} collective-permute-done((bf16[4,16,1024]{2,0,1:T(4,128)(2,1)S(1)}, bf16[4,16,1024]{2,0,1:T(4,128)(2,1)S(1)}, u32[]{:S(2)}, u32[]{:S(2)}) %collective-permute-start.3) | collective-permute-done | bytes 131104 | tf_op jit(solution)/shard_map/ppermute | solution.py:33
  336.8 5.5 %collective-permute-start.4 = (bf16[4,16,1024]{2,0,1:T(4,128)(2,1)S(1)}, bf16[4,16,1024]{2,0,1:T(4,128)(2,1)S(1)}, u32[]{:S(2)}, u32[]{:S(2)}) collective-permute-start(bf16[4,16,1024]{2,0,1:T(4,128)(2,1)S(1)} %get-tuple-element.964), channel_id=1, source_target_pairs={{0,8},{8,16},{16,24},{1,9},{9,17},{17,25},{2,10},{10,18},{18,26},{... | collective-permute-start | bytes 393224 | tf_op jit(solution)/shard_map/ppermute | solution.py:31
  346.6 5.0 %collective-permute-start.6 = (bf16[4,16,1024]{2,0,1:T(4,128)(2,1)S(1)}, bf16[4,16,1024]{2,0,1:T(4,128)(2,1)S(1)}, u32[]{:S(2)}, u32[]{:S(2)}) collective-permute-start(bf16[4,16,1024]{2,0,1:T(4,128)(2,1)S(1)} %get-tuple-element.950), channel_id=1, source_target_pairs={{0,8},{8,16},{16,24},{1,9},{9,17},{17,25},{2,10},{10,18},{18,26},{... | collective-permute-start | bytes 393224 | tf_op jit(solution)/shard_map/ppermute | solution.py:31
  357.0 8.0 %while.80 = (s32[]{:T(128)}, f32[8,4,8]{2,1,0:T(4,128)S(1)}, f32[8,4,8]{2,1,0:T(4,128)S(1)}, f32[8,4,8,128]{3,2,1,0:T(8,128)S(1)}, f32[8,8,4,8]{3,2,1,0:T(4,128)...) while((s32[]{:T(128)}, f32[8,4,8]{2,1,0:T(4,128)S(1)}, ...), condition=%wide.region_3.4_spmd, body=%wide.region_2.0_spmd.sunk | while | flops 99845 | bytes 403607 | solution.py:20
  366.0 8.0 %while.81 = (s32[]{:T(128)}, f32[8,4,8]{2,1,0:T(4,128)S(1)}, f32[8,4,8]{2,1,0:T(4,128)S(1)}, f32[8,4,8,128]{3,2,1,0:T(8,128)S(1)}, f32[8,8,4,8]{3,2,1,0:T(4,128)...) while((s32[]{:T(128)}, f32[8,4,8]{2,1,0:T(4,128)S(1)}, ...), condition=%wide.region_9.10_spmd, body=%wide.region_8.9_spmd.sunk | while | flops 99845 | bytes 403607 | solution.py:20
  374.9 8.0 %while.82 = (s32[]{:T(128)}, f32[8,4,8]{2,1,0:T(4,128)S(1)}, f32[8,4,8]{2,1,0:T(4,128)S(1)}, f32[8,4,8,128]{3,2,1,0:T(8,128)S(1)}, f32[8,8,4,8]{3,2,1,0:T(4,128)...) while((s32[]{:T(128)}, f32[8,4,8]{2,1,0:T(4,128)S(1)}, ...), condition=%wide.region_15.16_spmd, body=%wide.region_14.15_spmd.sunk | while | flops 99845 | bytes 403607 | solution.py:20
  385.0 8.0 %while.83 = (s32[]{:T(128)}, f32[8,4,8]{2,1,0:T(4,128)S(1)}, f32[8,4,8]{2,1,0:T(4,128)S(1)}, f32[8,4,8,128]{3,2,1,0:T(8,128)S(1)}, f32[8,8,4,8]{3,2,1,0:T(4,128)...) while((s32[]{:T(128)}, f32[8,4,8]{2,1,0:T(4,128)S(1)}, ...), condition=%wide.region_21.22_spmd, body=%wide.region_20.21_spmd.sunk | while | flops 99845 | bytes 403607 | solution.py:20
  (199 shorter events, 70.6 us)
Async XLA Ops:
  7.2 348.9 %all-gather.17.cloned.1.call-start = ((), (), s32[]{:S(2)}) async-start(), calls=%async_computation | async-start | bytes 1179648 | tf_op jit(solution)/shard_map/all_gather | solution.py:14
  51.4 1.3 copy-start
  54.3 310.7 %all-gather.19.cloned.1.call-start = ((), (), s32[]{:S(2)}) async-start(), calls=%async_computation.1 | async-start | bytes 1179648 | tf_op jit(solution)/shard_map/all_gather | solution.py:14
  56.5 1.3 copy-start.1
  59.5 314.5 %all-gather.21.cloned.1.call-start = ((), (), s32[]{:S(2)}) async-start(), calls=%async_computation.2 | async-start | bytes 1179648 | tf_op jit(solution)/shard_map/all_gather | solution.py:14
  61.7 1.3 copy-start.3
  63.0 1.6 copy-start.6
  63.0 1.7 copy-start.7
  64.6 319.4 %all-gather.23.cloned.1.call-start = ((), (), s32[]{:S(2)}) async-start(), calls=%async_computation.3 | async-start | bytes 1179648 | tf_op jit(solution)/shard_map/all_gather | solution.py:14
  64.8 259.7 %collective-permute-start = (bf16[4,16,1024]{2,0,1:T(4,128)(2,1)S(1)}, bf16[4,16,1024]{2,0,1:T(4,128)(2,1)S(1)}, u32[]{:S(2)}, u32[]{:S(2)}) collective-permute-start(bf16[4,16,1024]{2,0,1:T(4,128)(2,1)S(1)} %get-tuple-element.968), channel_id=1, source_target_pairs={{0,8},{8,16},{16,24},{1,9},{9,17},{17,25},{2,10},{10,18},{18,26},{... | collective-permute-start | bytes 393224 | tf_op jit(solution)/shard_map/ppermute | solution.py:31
  66.1 258.4 %collective-permute-start.1 = (bf16[4,16,1024]{2,0,1:T(4,128)(2,1)S(1)}, bf16[4,16,1024]{2,0,1:T(4,128)(2,1)}, u32[]{:S(2)}, u32[]{:S(2)}) collective-permute-start(bf16[4,16,1024]{2,0,1:T(4,128)(2,1)S(1)} %get-tuple-element.969), channel_id=1, source_target_pairs={{8,0},{16,8},{24,16},{9,1},{17,9},{25,17},{10,2},{18,10},{26,18},{... | collective-permute-start | bytes 393224 | tf_op jit(solution)/shard_map/ppermute | solution.py:33
  69.6 1.3 copy-start.4
  72.4 2.2 copy-start.2
  75.1 2.2 copy-start.5
  77.3 246.9 %copy-start.8 = (s32[4,8]{1,0:T(4,128)S(1)}, s32[4,8]{1,0:T(4,128)}, u32[]{:S(2)}) copy-start(s32[4,8]{1,0:T(4,128)} %param.25) | copy-start | bytes 388
  326.6 2.8 collective-permute-start.2
  327.9 7.7 %collective-permute-start.3 = (bf16[4,16,1024]{2,0,1:T(4,128)(2,1)S(1)}, bf16[4,16,1024]{2,0,1:T(4,128)(2,1)S(1)}, u32[]{:S(2)}, u32[]{:S(2)}) collective-permute-start(bf16[4,16,1024]{2,0,1:T(4,128)(2,1)S(1)} %get-tuple-element.967), channel_id=1, source_target_pairs={{8,0},{16,8},{24,16},{9,1},{17,9},{25,17},{10,2},{18,10},{26,18},{... | collective-permute-start | bytes 393224 | tf_op jit(solution)/shard_map/ppermute | solution.py:33
  336.8 7.2 %collective-permute-start.4 = (bf16[4,16,1024]{2,0,1:T(4,128)(2,1)S(1)}, bf16[4,16,1024]{2,0,1:T(4,128)(2,1)S(1)}, u32[]{:S(2)}, u32[]{:S(2)}) collective-permute-start(bf16[4,16,1024]{2,0,1:T(4,128)(2,1)S(1)} %get-tuple-element.964), channel_id=1, source_target_pairs={{0,8},{8,16},{16,24},{1,9},{9,17},{17,25},{2,10},{10,18},{18,26},{... | collective-permute-start | bytes 393224 | tf_op jit(solution)/shard_map/ppermute | solution.py:31
  342.2 3.2 collective-permute-start.5
  346.6 6.5 %collective-permute-start.6 = (bf16[4,16,1024]{2,0,1:T(4,128)(2,1)S(1)}, bf16[4,16,1024]{2,0,1:T(4,128)(2,1)S(1)}, u32[]{:S(2)}, u32[]{:S(2)}) collective-permute-start(bf16[4,16,1024]{2,0,1:T(4,128)(2,1)S(1)} %get-tuple-element.950), channel_id=1, source_target_pairs={{0,8},{8,16},{16,24},{1,9},{9,17},{17,25},{2,10},{10,18},{18,26},{... | collective-permute-start | bytes 393224 | tf_op jit(solution)/shard_map/ppermute | solution.py:31
  351.6 3.2 collective-permute-start.7
Sparse Core Ops, SparseCore 0:
  54.5 41.2 all-gather.16
  98.0 39.8 all-gather.18
  140.1 39.3 all-gather.20
  181.5 39.7 all-gather.22
where the time goes:
time: 404 us; the launch traced here: 401 us
  blocking collectives  278 us (69%)
  other arithmetic  38.8 us (10%)
  local copies, waits for them, and re-layouts  21.2 us (5%)
  matrix products  19.2 us (5%)
  starting transfers between devices  18.5 us (5%)
  between operations  14.4 us (4%)
  waiting for transfers between devices  9.49 us (2%)
    all_gather x8, blocking collectives, joined(): everything = jax.tree.map(lambda part: lax.all_gather(part, axis), array)  246 us
    all_gather x1, blocking collectives, shards(): every_query = lax.all_gather(queries, 'ctx', axis=2, tiled=True)  32.7 us
    add x28, other arithmetic, merge_softmax(): first_sum * first_factor[..., None] + second_sum * second_factor[..., None]  30.1 us
    ppermute x4, starting transfers between devices, extended_2(): lax.ppermute(tail, axis, [(i, (i + 1) % count) for i in range(ends)])  13 us
    unnamed x22, local copies, waits for them, and re-layouts  11.6 us
    ppermute x4, waiting for transfers between devices, extended_2(): lax.ppermute(head, axis, [((i + 1) % count, i) for i in range(ends)])  9.35 us
    dot_general x4, matrix products, shards(): jnp.einsum('pged,tgd->pget', query_heads, prompt_keys, preferred_element_...  8.54 us
  transfers between devices with their start and end apart: 12, of which 3 were waited for; matrix products, arithmetic and copies ran while one was open for 13% of the time, Pallas kernels for 0%

commit v1 on v0

v1 whole, which is shorter than its diff:
```python
import functools

import jax
import jax.numpy as jnp
from jax import lax
from jax.experimental import pallas as pl
from jax.experimental.pallas import tpu as pltpu
from jax.sharding import PartitionSpec as P

HEADS = 32
HEAD_DIM = 128
MESH = pl.DeviceIdType.MESH
LOG2E = 1.4426950408889634
FLOOR = -1e30
LANES = 128
SPAN = 2
FAR = (-1, 1, -2, 2)


def nt(a, b):
    return lax.dot_general(a, b, (((1,), (1,)), ((), ())), preferred_element_type=jnp.float32)


def nn(a, b):
    return jnp.dot(a, b, preferred_element_type=jnp.float32)


def kernel(
    n_ctx, n_dom, key_heads, steps, history,
    kv_ref, cache_ref, q_ref, anc_ref,
    att_ref, out_ref,
    k_buf, v_buf, q_all, part, got, window, anc_win,
    kv_sem, q_send, q_recv, p_send, p_recv, w_send, w_recv, a_send, a_recv,
):
    column = lax.axis_index("ctx")
    row = lax.axis_index("dom")
    own = HEADS // n_ctx
    members = n_ctx // key_heads
    my_head = column // members
    my_member = column % members
    parts = q_ref.shape[1]
    slots = history + steps
    moments = steps * parts
    rows = own * moments
    key_width = key_heads * HEAD_DIM
    factor = LOG2E / HEAD_DIM**0.5

    def head_at(i):
        return lax.rem(my_head + i, key_heads)

    def loads(i):
        e = head_at(i)
        at = pl.multiple_of(e * HEAD_DIM, HEAD_DIM)
        return (
            pltpu.make_async_copy(kv_ref.at[:, pl.ds(at, HEAD_DIM)], k_buf.at[i], kv_sem.at[i, 0]),
            pltpu.make_async_copy(
                kv_ref.at[:, pl.ds(at + key_width, HEAD_DIM)], v_buf.at[i], kv_sem.at[i, 1]
            ),
        )

    for i in range(key_heads):
        for copy in loads(i):
            copy.start()

    barrier = pltpu.get_barrier_semaphore()
    for o in range(1, n_ctx):
        pl.semaphore_signal(
            barrier, inc=1, device_id={"ctx": lax.rem(column + o, n_ctx)}, device_id_type=MESH
        )

    def inside(delta):
        return (row + delta >= 0) & (row + delta < n_dom)

    for delta in FAR:
        @pl.when(inside(delta))
        def _():
            pl.semaphore_signal(barrier, inc=1, device_id={"dom": row + delta}, device_id_type=MESH)

    wide = jnp.concatenate([q_ref[s].astype(jnp.float32) for s in range(steps)], axis=0)
    mine = jnp.concatenate(
        [wide[:, h * HEAD_DIM : (h + 1) * HEAD_DIM] for h in range(own)], axis=0
    ).astype(jnp.bfloat16)
    q_all[column] = mine
    lane = lax.broadcasted_iota(jnp.int32, (steps, LANES), 1)
    tile = jnp.full((steps, LANES), -1, jnp.int32)
    anc = anc_ref[...]
    for p in range(parts):
        tile = jnp.where(lane == lax.rem(row * parts + p, LANES), anc[:, p : p + 1], tile)
    anc_win[SPAN] = jnp.concatenate([tile, jnp.full((8 - steps, LANES), -1, jnp.int32)], axis=0)
    for delta in FAR:
        @pl.when(jnp.logical_not(inside(delta)))
        def _():
            anc_win[SPAN + delta] = jnp.full((8, LANES), -1, jnp.int32)
            window[SPAN + delta] = jnp.zeros(window.shape[1:], window.dtype)

    near = jnp.minimum(row, SPAN) + jnp.minimum(n_dom - 1 - row, SPAN)
    pl.semaphore_wait(barrier, n_ctx - 1 + near)

    def q_copy(peer, source):
        return pltpu.make_async_remote_copy(
            src_ref=q_all.at[source], dst_ref=q_all.at[source],
            send_sem=q_send.at[peer], recv_sem=q_recv.at[source],
            device_id={"ctx": peer}, device_id_type=MESH,
        )

    def peers_of(i):
        e = lax.rem(my_head + key_heads - i, key_heads)
        first = 1 if i == 0 else 0
        return [e * members + lax.rem(my_member + o, members) for o in range(first, members)]

    for i in range(key_heads):
        for peer in peers_of(i):
            q_copy(peer, column).start()

    def w_copy(delta):
        return pltpu.make_async_remote_copy(
            src_ref=cache_ref, dst_ref=window.at[SPAN - delta],
            send_sem=w_send.at[SPAN + delta], recv_sem=w_recv.at[SPAN - delta],
            device_id={"dom": row + delta}, device_id_type=MESH,
        )

    def a_copy(delta):
        return pltpu.make_async_remote_copy(
            src_ref=anc_win.at[SPAN], dst_ref=anc_win.at[SPAN - delta],
            send_sem=a_send.at[SPAN + delta], recv_sem=a_recv.at[SPAN - delta],
            device_id={"dom": row + delta}, device_id_type=MESH,
        )

    def w_arrival(delta):
        return pltpu.make_async_remote_copy(
            src_ref=cache_ref, dst_ref=window.at[SPAN + delta],
            send_sem=w_send.at[SPAN - delta], recv_sem=w_recv.at[SPAN + delta],
            device_id={"dom": row + delta}, device_id_type=MESH,
        )

    def a_arrival(delta):
        return pltpu.make_async_remote_copy(
            src_ref=anc_win.at[SPAN], dst_ref=anc_win.at[SPAN + delta],
            send_sem=a_send.at[SPAN - delta], recv_sem=a_recv.at[SPAN + delta],
            device_id={"dom": row + delta}, device_id_type=MESH,
        )

    for delta in FAR:
        @pl.when(inside(delta))
        def _():
            a_copy(delta).start()
            w_copy(delta).start()

    window[SPAN] = cache_ref[...]

    def p_copy(peer, source):
        return pltpu.make_async_remote_copy(
            src_ref=part.at[peer], dst_ref=got.at[source],
            send_sem=p_send.at[peer], recv_sem=p_recv.at[source],
            device_id={"ctx": peer}, device_id_type=MESH,
        )

    def stats_tile(m, l):
        n = m.shape[0]
        li = lax.broadcasted_iota(jnp.int32, (n, LANES), 1)
        both = jnp.where(li == 0, m, jnp.where(li == 1, l, 0.0))
        turned = jnp.transpose(both)[:8]
        if n < LANES:
            turned = jnp.concatenate([turned, jnp.zeros((8, LANES - n), jnp.float32)], axis=1)
        return turned

    for i in range(key_heads):
        e = head_at(i)
        for copy in loads(i):
            copy.wait()
        for o in range(1 if i == 0 else 0, members):
            source = e * members + lax.rem(my_member + o, members)
            q_copy(source, source).wait_recv()
        q = q_all[pl.ds(e * members, members)].reshape(members * rows, HEAD_DIM)
        score = nt(q, k_buf[i])
        peak = jnp.max(score, axis=1, keepdims=True) * factor
        weight = jnp.exp2(score * factor - peak)
        total = jnp.sum(weight, axis=1, keepdims=True)
        summed = nn(weight.astype(jnp.bfloat16), v_buf[i])
        for m in range(members):
            peer = e * members + m
            cut = slice(m * rows, (m + 1) * rows)
            part[peer, :rows] = summed[cut]
            part[peer, rows:] = stats_tile(peak[cut], total[cut])
            if i == 0:
                @pl.when(m != my_member)
                def _():
                    p_copy(peer, column).start()
            else:
                p_copy(peer, column).start()

    for delta in FAR:
        @pl.when(inside(delta))
        def _():
            a_arrival(delta).wait_recv()
    known = anc_win[0]
    for w in range(1, 2 * SPAN + 1):
        known = jnp.maximum(known, anc_win[w])
    known = jnp.where(known >= 0, lax.rem(known, LANES), -1)
    q_id = lax.broadcasted_iota(jnp.int32, (LANES, LANES), 0)
    one = lax.broadcasted_iota(jnp.int32, (parts, LANES), 1) == lax.rem(
        row * parts + lax.broadcasted_iota(jnp.int32, (parts, LANES), 0), LANES
    )
    one = one.astype(jnp.float32)
    zero = jnp.zeros_like(one)
    origin = {}
    for k in range(steps - 1, -1, -1):
        origin[k, k] = one
        start = [origin[s, k + 1] for s in range(k + 1, steps + 1) if s != k + 1] + [one]
        names = list(range(k + 2, steps + 1)) + [k + 1]
        turn = (known[k : k + 1, :] == q_id).astype(jnp.float32).astype(jnp.bfloat16)
        moved = nt(jnp.concatenate(start, axis=0).astype(jnp.bfloat16), turn)
        for n, s in enumerate(names):
            origin[s, k] = moved[n * parts : (n + 1) * parts]
    stack = jnp.concatenate(
        [origin.get((s, k), zero) if s >= k else zero for k in range(steps) for s in range(steps + 1)],
        axis=0,
    ).astype(jnp.bfloat16)
    cols = (2 * SPAN + 1) * parts * slots
    block = (steps + 1) * parts
    col = lax.broadcasted_iota(jnp.int32, (LANES, cols), 1)
    particle = lax.rem((row - SPAN) * parts + col // slots + 16 * LANES, LANES)
    spread = (particle == lax.broadcasted_iota(jnp.int32, (LANES, cols), 0)).astype(
        jnp.float32
    ).astype(jnp.bfloat16)
    from_where = nn(stack, spread)
    slot = lax.rem(lax.broadcasted_iota(jnp.int32, (block, cols), 1), slots)
    kind = jnp.maximum(slot - history, 0)
    valid = jnp.zeros((block, cols), jnp.float32)
    for k in range(steps):
        valid = jnp.where(kind == k, from_where[k * block : (k + 1) * block], valid)

    for delta in FAR:
        @pl.when(inside(delta))
        def _():
            w_arrival(delta).wait_recv()

    pick = jnp.broadcast_to(valid[moments:, None, :], (parts, slots, cols)).reshape(parts * slots, cols)
    same = lax.rem(lax.broadcasted_iota(jnp.int32, (parts * slots, cols), 1), slots) == lax.rem(
        lax.broadcasted_iota(jnp.int32, (parts * slots, cols), 0), slots
    )
    pick = jnp.where(same, pick, 0.0).astype(jnp.bfloat16)
    for c in range(0, 2 * key_width, 256):
        piece = window[:, :, c : c + 256].reshape(cols, 256)
        out_ref[:, c : c + 256] = nn(pick, piece).astype(jnp.bfloat16)

    at = pl.multiple_of(my_head * HEAD_DIM, HEAD_DIM)
    keys = window[:, :, pl.ds(at, HEAD_DIM)].reshape(cols, HEAD_DIM)
    vals = window[:, :, pl.ds(pl.multiple_of(at + key_width, HEAD_DIM), HEAD_DIM)].reshape(
        cols, HEAD_DIM
    )
    allowed = jnp.concatenate([valid[:moments]] * own, axis=0) > 0.5
    score = jnp.where(allowed, nt(q_all[column], keys) * factor, FLOOR)
    peak = jnp.max(score, axis=1, keepdims=True)
    weight = jnp.where(allowed, jnp.exp2(score - peak), 0.0)
    total = jnp.sum(weight, axis=1, keepdims=True)
    summed = nn(weight.astype(jnp.bfloat16), vals)

    for o in range(1, n_ctx):
        source = lax.rem(column + o, n_ctx)
        p_copy(source, source).wait_recv()
    peaks, totals, sums = [peak], [total], [summed]
    for o in range(n_ctx):
        source = lax.rem(column + o, n_ctx)
        whole = part.at[column] if o == 0 else got.at[source]
        stats = jnp.transpose(
            jnp.concatenate([whole[rows:], jnp.zeros((LANES - 8, LANES), jnp.float32)], axis=0)
        )[:rows]
        peaks.append(stats[:, 0:1])
        totals.append(stats[:, 1:2])
        sums.append(whole[:rows])
    highest = functools.reduce(jnp.maximum, peaks)
    bottom, top = 0.0, 0.0
    for m, l, s in zip(peaks, totals, sums):
        scale = jnp.exp2(m - highest)
        bottom = bottom + l * scale
        top = top + s * scale
    result = top / bottom
    for h in range(own):
        for s in range(steps):
            at = h * moments + s * parts
            att_ref[s, :, h * HEAD_DIM : (h + 1) * HEAD_DIM] = result[at : at + parts]

    for o in range(1, n_ctx):
        peer = lax.rem(column + o, n_ctx)
        q_copy(peer, column).wait_send()
        p_copy(peer, column).wait_send()
    for delta in FAR:
        @pl.when(inside(delta))
        def _():
            a_copy(delta).wait_send()
            w_copy(delta).wait_send()


def solution(mesh):
    n_ctx, n_dom = mesh.shape["ctx"], mesh.shape["dom"]

    def shards(prompt_kv, suffix_kv, new_kv, queries, ancestors):
        parts, history, width = suffix_kv.shape
        steps = queries.shape[0]
        key_heads = width // (2 * HEAD_DIM)
        slots = history + steps
        positions = prompt_kv.shape[0]
        own = HEADS // n_ctx
        rows = own * steps * parts
        cache = jnp.concatenate([suffix_kv, jnp.transpose(new_kv, (1, 0, 2))], axis=1)
        cache = cache.reshape(parts * slots, width)
        vmem = pl.BlockSpec(memory_space=pltpu.VMEM)
        dma = pltpu.SemaphoreType.DMA
        attended, suffix_out = pl.pallas_call(
            functools.partial(kernel, n_ctx, n_dom, key_heads, steps, history),
            out_shape=(
                jax.ShapeDtypeStruct((steps, parts, own * HEAD_DIM), jnp.float32),
                jax.ShapeDtypeStruct((parts * slots, width), jnp.bfloat16),
            ),
            in_specs=[pl.BlockSpec(memory_space=pl.ANY), vmem, vmem, vmem],
            out_specs=(vmem, vmem),
            scratch_shapes=[
                pltpu.VMEM((key_heads, positions, HEAD_DIM), jnp.bfloat16),
                pltpu.VMEM((key_heads, positions, HEAD_DIM), jnp.bfloat16),
                pltpu.VMEM((n_ctx, rows, HEAD_DIM), jnp.bfloat16),
                pltpu.VMEM((n_ctx, rows + 8, HEAD_DIM), jnp.float32),
                pltpu.VMEM((n_ctx, rows + 8, HEAD_DIM), jnp.float32),
                pltpu.VMEM((2 * SPAN + 1, parts * slots, width), jnp.bfloat16),
                pltpu.VMEM((2 * SPAN + 1, 8, LANES), jnp.int32),
                dma((key_heads, 2)),
                dma((n_ctx,)), dma((n_ctx,)), dma((n_ctx,)), dma((n_ctx,)),
                dma((2 * SPAN + 1,)), dma((2 * SPAN + 1,)),
                dma((2 * SPAN + 1,)), dma((2 * SPAN + 1,)),
            ],
            compiler_params=pltpu.CompilerParams(
                collective_id=0, has_side_effects=True, vmem_limit_bytes=48 * 1024 * 1024
            ),
            cost_estimate=pl.CostEstimate(
                flops=4 * HEADS * steps * parts * positions * HEAD_DIM,
                bytes_accessed=4 * positions * width,
                transcendentals=HEADS * steps * parts * positions,
            ),
        )(prompt_kv, cache, queries, ancestors)
        return attended, suffix_out.reshape(parts, slots, width)

    return jax.shard_map(
        shards,
        mesh=mesh,
        in_specs=(
            P("ctx", None),
            P("dom", None, None),
            P(None, "dom", None),
            P(None, "dom", "ctx"),
            P(None, "dom"),
        ),
        out_specs=(P(None, "dom", "ctx"), P("dom", None, None)),
        check_vma=False,
    )
```

time: 404 us -> 32.3 us (0.08)
  the two profiles are of different devices: /device:TPU:0 before, /device:TPU:15 now
where the time goes in v1:
time: 32.3 us; the launch traced here: 32.1 us
  Pallas kernels  25.3 us (78%)
  local copies, waits for them, and re-layouts  5.11 us (16%)
  other arithmetic  0.99 us (3%)
  between operations  0.66 us (2%)
    pallas_call x1, Pallas kernels, shards(): pl.pallas_call(functools.partial(kernel, n_ctx, n_dom, key_heads, steps,...  25.3 us
    unnamed x8, local copies, waits for them, and re-layouts  4.96 us
    concatenate x1, other arithmetic, shards(): jnp.concatenate([suffix_kv, jnp.transpose(new_kv, (1, 0, 2))], axis=1)  0.99 us

profile of v1, /device:TPU:15, one launch (start us, length us, event | category | flops | bytes accessed | tf_op | source)
XLA Modules:
  0.0 32.1 jit_solution(3468060345580168289)
XLA Ops:
  0.6 1.0 %pad_maximum_fusion = bf16[8,16,1024]{2,0,1:T(8,128)(2,1)S(1)} fusion(bf16[8,4,1024]{2,0,1:T(8,128)(2,1)} %bitcast.5, bf16[8,12,1024]{2,0,1:T(8,128)(2,1)} %param.6), kind=kLoop, calls=%fused_computation | loop fusion | flops 131072 | bytes 524288 | tf_op jit(solution)/shard_map/concatenate | solution.py:306
  1.6 0.2 copy.7
  1.8 0.0 copy-start
  1.8 2.2 %copy-done = bf16[2048,1024]{1,0:T(8,128)(2,1)S(1)} copy-done((bf16[2048,1024]{1,0:T(8,128)(2,1)S(1)}, bf16[2048,1024]{1,0:T(8,128)(2,1)}, u32[]{:S(2)}) %copy-start) | copy-done | bytes 4194328
  4.0 0.0 copy-start.1
  4.0 0.8 %copy-done.1 = bf16[4,8,512]{2,1,0:T(8,128)(2,1)S(1)} copy-done((bf16[4,8,512]{2,1,0:T(8,128)(2,1)S(1)}, bf16[4,8,512]{2,1,0:T(8,128)(2,1)}, u32[]{:S(2)}) %copy-start.1) | copy-done | bytes 32792
  4.7 0.0 copy-start.2
  4.7 0.7 %copy-done.2 = s32[4,8]{1,0:T(4,128)S(1)} copy-done((s32[4,8]{1,0:T(4,128)S(1)}, s32[4,8]{1,0:T(4,128)}, u32[]{:S(2)}) %copy-start.2) | copy-done | bytes 152
  5.4 25.3 %shard_map.68 = (f32[4,8,512]{2,1,0:T(8,128)S(1)}, bf16[128,1024]{1,0:T(8,128)(2,1)S(1)}) custom-call(bf16[2048,1024]{1,0:T(8,128)(2,1)S(1)} %copy-done, bf16[128,1024]{1,0:T(8,128)(2,1)S(1)} %bitcast.3, bf16[4,8,512]{2,1,0:T(8,128)(2,1)S(1)} %copy-done.1, s32[4,8]{1,0:T(4,128)S(1)} %copy-done.2), custom_call_target="tpu_custom_call" | custom-call | flops 1073741824 | bytes 8388608 | tf_op jit(solution)/shard_map/pallas_call | solution.py:310
  30.7 0.6 %copy.10 = f32[4,8,512]{2,1,0:T(8,128)} copy(f32[4,8,512]{2,1,0:T(8,128)S(1)} %get-tuple-element.8) | data formatting | bytes 131072
  31.4 0.7 %copy.11 = bf16[8,16,1024]{2,1,0:T(8,128)(2,1)} copy(bf16[8,16,1024]{2,1,0:T(8,128)(2,1)S(1)} %bitcast.4) | data formatting | bytes 524288
Async XLA Ops:
  1.8 2.2 %copy-start = (bf16[2048,1024]{1,0:T(8,128)(2,1)S(1)}, bf16[2048,1024]{1,0:T(8,128)(2,1)}, u32[]{:S(2)}) copy-start(bf16[2048,1024]{1,0:T(8,128)(2,1)} %kv_ref.1) | copy-start | bytes 12582916
  4.0 0.8 %copy-start.1 = (bf16[4,8,512]{2,1,0:T(8,128)(2,1)S(1)}, bf16[4,8,512]{2,1,0:T(8,128)(2,1)}, u32[]{:S(2)}) copy-start(bf16[4,8,512]{2,1,0:T(8,128)(2,1)} %q_ref.1) | copy-start | bytes 98308
  4.7 0.7 %copy-start.2 = (s32[4,8]{1,0:T(4,128)S(1)}, s32[4,8]{1,0:T(4,128)}, u32[]{:S(2)}) copy-start(s32[4,8]{1,0:T(4,128)} %anc_ref.1) | copy-start | bytes 388

commit v2 on v1

--- a/solution.py
+++ b/solution.py
@@ -13,6 +13,8 @@
 LOG2E = 1.4426950408889634
 FLOOR = -1e30
 LANES = 128
+CODES = 32767.0
+TINY = 1e-30
 SPAN = 2
 FAR = (-1, 1, -2, 2)
 
@@ -27,10 +29,11 @@
 
 def kernel(
     n_ctx, n_dom, key_heads, steps, history,
-    kv_ref, cache_ref, q_ref, anc_ref,
+    kv_ref, old_ref, new_ref, q_ref, anc_ref,
     att_ref, out_ref,
-    k_buf, v_buf, q_all, part, got, window, anc_win,
-    kv_sem, q_send, q_recv, p_send, p_recv, w_send, w_recv, a_send, a_recv,
+    k_buf, v_buf, q_raw, anc_raw, q_all, part, got, part_stats, got_stats, window, anc_win,
+    kv_sem, in_sem, q_send, q_recv, r_send, p_send, p_recv, t_send, t_recv,
+    w_send, w_recv, n_send, n_recv, a_send, a_recv,
 ):
     column = lax.axis_index("ctx")
     row = lax.axis_index("dom")
@@ -45,8 +48,25 @@
     key_width = key_heads * HEAD_DIM
     factor = LOG2E / HEAD_DIM**0.5
 
+    pair = column + 1 - 2 * (column % 2)
+    order = [0] + sorted(range(1, key_heads), key=lambda i: (i < key_heads // 2, i))
+
     def head_at(i):
-        return lax.rem(my_head + i, key_heads)
+        e, bit = my_head, 1
+        while bit < key_heads:
+            if i & bit:
+                e = e + bit - 2 * bit * (my_head // bit % 2)
+            bit *= 2
+        return e
+
+    def same_side(i):
+        e = head_at(i)
+        half = members // 2
+        mine = my_member // 2
+        first = 1 if i == 0 else 0
+        return [
+            e * members + 2 * lax.rem(mine + o, half) + my_member % 2 for o in range(first, half)
+        ]
 
     def loads(i):
         e = head_at(i)
@@ -58,9 +78,20 @@
             ),
         )
 
-    for i in range(key_heads):
+    q_in = pltpu.make_async_copy(q_ref, q_raw, in_sem.at[0])
+    anc_in = pltpu.make_async_copy(anc_ref, anc_raw, in_sem.at[1])
+    old_rows, new_rows = old_ref.shape[0], new_ref.shape[0]
+    old_in = pltpu.make_async_copy(old_ref, window.at[SPAN, pl.ds(0, old_rows)], in_sem.at[2])
+    new_in = pltpu.make_async_copy(
+        new_ref, window.at[SPAN, pl.ds(old_rows, new_rows)], in_sem.at[3]
+    )
+    q_in.start()
+    anc_in.start()
+    for i in order:
         for copy in loads(i):
             copy.start()
+    old_in.start()
+    new_in.start()
 
     barrier = pltpu.get_barrier_semaphore()
     for o in range(1, n_ctx):
@@ -76,14 +107,16 @@
         def _():
             pl.semaphore_signal(barrier, inc=1, device_id={"dom": row + delta}, device_id_type=MESH)
 
-    wide = jnp.concatenate([q_ref[s].astype(jnp.float32) for s in range(steps)], axis=0)
+    q_in.wait()
+    anc_in.wait()
+    wide = jnp.concatenate([q_raw[s].astype(jnp.float32) for s in range(steps)], axis=0)
     mine = jnp.concatenate(
         [wide[:, h * HEAD_DIM : (h + 1) * HEAD_DIM] for h in range(own)], axis=0
     ).astype(jnp.bfloat16)
     q_all[column] = mine
     lane = lax.broadcasted_iota(jnp.int32, (steps, LANES), 1)
     tile = jnp.full((steps, LANES), -1, jnp.int32)
-    anc = anc_ref[...]
+    anc = anc_raw[...]
     for p in range(parts):
         tile = jnp.where(lane == lax.rem(row * parts + p, LANES), anc[:, p : p + 1], tile)
     anc_win[SPAN] = jnp.concatenate([tile, jnp.full((8 - steps, LANES), -1, jnp.int32)], axis=0)
@@ -96,28 +129,40 @@
     near = jnp.minimum(row, SPAN) + jnp.minimum(n_dom - 1 - row, SPAN)
     pl.semaphore_wait(barrier, n_ctx - 1 + near)
 
-    def q_copy(peer, source):
+    def q_copy(peer, source, sems):
         return pltpu.make_async_remote_copy(
             src_ref=q_all.at[source], dst_ref=q_all.at[source],
-            send_sem=q_send.at[peer], recv_sem=q_recv.at[source],
+            send_sem=sems, recv_sem=q_recv.at[source],
             device_id={"ctx": peer}, device_id_type=MESH,
         )
 
-    def peers_of(i):
-        e = lax.rem(my_head + key_heads - i, key_heads)
-        first = 1 if i == 0 else 0
-        return [e * members + lax.rem(my_member + o, members) for o in range(first, members)]
-
-    for i in range(key_heads):
-        for peer in peers_of(i):
-            q_copy(peer, column).start()
-
-    def w_copy(delta):
-        return pltpu.make_async_remote_copy(
-            src_ref=cache_ref, dst_ref=window.at[SPAN - delta],
-            send_sem=w_send.at[SPAN + delta], recv_sem=w_recv.at[SPAN - delta],
-            device_id={"dom": row + delta}, device_id_type=MESH,
-        )
+    def relay(i):
+        for source in same_side(i):
+            q_copy(source, source, q_send.at[source]).wait_recv()
+            q_copy(pair, source, r_send.at[source]).start()
+
+    q_copy(pair, column, r_send.at[column]).start()
+    for i in order:
+        for peer in same_side(i):
+            q_copy(peer, column, q_send.at[peer]).start()
+
+    def w_pieces(delta, at, sent, landed):
+        return [
+            pltpu.make_async_remote_copy(
+                src_ref=source, dst_ref=window.at[SPAN + at, pl.ds(first, source.shape[0])],
+                send_sem=send.at[SPAN + sent], recv_sem=recv.at[SPAN + landed],
+                device_id={"dom": row + delta}, device_id_type=MESH,
+            )
+            for source, first, send, recv in (
+                (old_ref, 0, w_send, w_recv), (new_ref, old_rows, n_send, n_recv)
+            )
+        ]
+
+    def w_copies(delta):
+        return w_pieces(delta, -delta, delta, -delta)
+
+    def w_arrivals(delta):
+        return w_pieces(delta, delta, -delta, delta)
 
     def a_copy(delta):
         return pltpu.make_async_remote_copy(
@@ -126,13 +171,6 @@
             device_id={"dom": row + delta}, device_id_type=MESH,
         )
 
-    def w_arrival(delta):
-        return pltpu.make_async_remote_copy(
-            src_ref=cache_ref, dst_ref=window.at[SPAN + delta],
-            send_sem=w_send.at[SPAN - delta], recv_sem=w_recv.at[SPAN + delta],
-            device_id={"dom": row + delta}, device_id_type=MESH,
-        )
-
     def a_arrival(delta):
         return pltpu.make_async_remote_copy(
             src_ref=anc_win.at[SPAN], dst_ref=anc_win.at[SPAN + delta],
@@ -144,50 +182,66 @@
         @pl.when(inside(delta))
         def _():
             a_copy(delta).start()
-            w_copy(delta).start()
-
-    window[SPAN] = cache_ref[...]
-
-    def p_copy(peer, source):
-        return pltpu.make_async_remote_copy(
-            src_ref=part.at[peer], dst_ref=got.at[source],
-            send_sem=p_send.at[peer], recv_sem=p_recv.at[source],
-            device_id={"ctx": peer}, device_id_type=MESH,
-        )
-
-    def stats_tile(m, l):
-        n = m.shape[0]
+            for copy in w_copies(delta):
+                copy.start()
+
+    def p_copies(peer, source):
+        return [
+            pltpu.make_async_remote_copy(
+                src_ref=mine.at[peer], dst_ref=theirs.at[source],
+                send_sem=send.at[peer], recv_sem=recv.at[source],
+                device_id={"ctx": peer}, device_id_type=MESH,
+            )
+            for mine, theirs, send, recv in (
+                (part_stats, got_stats, t_send, t_recv), (part, got, p_send, p_recv)
+            )
+        ]
+
+    def stats_tile(*columns):
+        n = columns[0].shape[0]
         li = lax.broadcasted_iota(jnp.int32, (n, LANES), 1)
-        both = jnp.where(li == 0, m, jnp.where(li == 1, l, 0.0))
+        both = jnp.zeros((n, LANES), jnp.float32)
+        for at, value in enumerate(columns):
+            both = jnp.where(li == at, value, both)
         turned = jnp.transpose(both)[:8]
         if n < LANES:
             turned = jnp.concatenate([turned, jnp.zeros((8, LANES - n), jnp.float32)], axis=1)
         return turned
 
-    for i in range(key_heads):
+    relay(0)
+    relay(order[1])
+    for n, i in enumerate(order):
         e = head_at(i)
         for copy in loads(i):
             copy.wait()
-        for o in range(1 if i == 0 else 0, members):
-            source = e * members + lax.rem(my_member + o, members)
-            q_copy(source, source).wait_recv()
+        for o in range(members // 2):
+            source = e * members + 2 * o + pair % 2
+            q_copy(source, source, q_send.at[source]).wait_recv()
         q = q_all[pl.ds(e * members, members)].reshape(members * rows, HEAD_DIM)
         score = nt(q, k_buf[i])
         peak = jnp.max(score, axis=1, keepdims=True) * factor
         weight = jnp.exp2(score * factor - peak)
         total = jnp.sum(weight, axis=1, keepdims=True)
         summed = nn(weight.astype(jnp.bfloat16), v_buf[i])
+        largest = jnp.max(jnp.abs(summed), axis=1, keepdims=True)
+        coded = jnp.round(summed * (CODES / jnp.maximum(largest, TINY))).astype(jnp.int32)
+        coded = coded.astype(jnp.int16)
         for m in range(members):
             peer = e * members + m
             cut = slice(m * rows, (m + 1) * rows)
-            part[peer, :rows] = summed[cut]
-            part[peer, rows:] = stats_tile(peak[cut], total[cut])
+            part[peer] = coded[cut]
+            part_stats[peer] = stats_tile(peak[cut], total[cut], largest[cut])
             if i == 0:
                 @pl.when(m != my_member)
                 def _():
-                    p_copy(peer, column).start()
+                    for copy in p_copies(peer, column):
+                        copy.start()
             else:
-                p_copy(peer, column).start()
+                for copy in p_copies(peer, column):
+                    copy.start()
+        if n == 0:
+            for later in order[2:]:
+                relay(later)
 
     for delta in FAR:
         @pl.when(inside(delta))
@@ -219,12 +273,14 @@
     cols = (2 * SPAN + 1) * parts * slots
     block = (steps + 1) * parts
     col = lax.broadcasted_iota(jnp.int32, (LANES, cols), 1)
-    particle = lax.rem((row - SPAN) * parts + col // slots + 16 * LANES, LANES)
+    particle = lax.rem(
+        (row - SPAN + col // (parts * slots)) * parts + col % parts + 16 * LANES, LANES
+    )
     spread = (particle == lax.broadcasted_iota(jnp.int32, (LANES, cols), 0)).astype(
         jnp.float32
     ).astype(jnp.bfloat16)
     from_where = nn(stack, spread)
-    slot = lax.rem(lax.broadcasted_iota(jnp.int32, (block, cols), 1), slots)
+    slot = lax.broadcasted_iota(jnp.int32, (block, cols), 1) // parts % slots
     kind = jnp.maximum(slot - history, 0)
     valid = jnp.zeros((block, cols), jnp.float32)
     for k in range(steps):
@@ -233,10 +289,13 @@
     for delta in FAR:
         @pl.when(inside(delta))
         def _():
-            w_arrival(delta).wait_recv()
+            for copy in w_arrivals(delta):
+                copy.wait_recv()
+    old_in.wait()
+    new_in.wait()
 
     pick = jnp.broadcast_to(valid[moments:, None, :], (parts, slots, cols)).reshape(parts * slots, cols)
-    same = lax.rem(lax.broadcasted_iota(jnp.int32, (parts * slots, cols), 1), slots) == lax.rem(
+    same = lax.broadcasted_iota(jnp.int32, (parts * slots, cols), 1) // parts % slots == lax.rem(
         lax.broadcasted_iota(jnp.int32, (parts * slots, cols), 0), slots
     )
     pick = jnp.where(same, pick, 0.0).astype(jnp.bfloat16)
@@ -258,38 +317,47 @@
 
     for o in range(1, n_ctx):
         source = lax.rem(column + o, n_ctx)
-        p_copy(source, source).wait_recv()
-    peaks, totals, sums = [peak], [total], [summed]
+        for copy in p_copies(source, source):
+            copy.wait_recv()
+    peaks, totals, scales, sums = [peak], [total], [1.0], [summed]
     for o in range(n_ctx):
         source = lax.rem(column + o, n_ctx)
-        whole = part.at[column] if o == 0 else got.at[source]
+        codes = part[column] if o == 0 else got[source]
+        tile = part_stats[column] if o == 0 else got_stats[source]
         stats = jnp.transpose(
-            jnp.concatenate([whole[rows:], jnp.zeros((LANES - 8, LANES), jnp.float32)], axis=0)
+            jnp.concatenate([tile, jnp.zeros((LANES - 8, LANES), jnp.float32)], axis=0)
         )[:rows]
         peaks.append(stats[:, 0:1])
         totals.append(stats[:, 1:2])
-        sums.append(whole[:rows])
+        scales.append(stats[:, 2:3] * (1.0 / CODES))
+        sums.append(codes.astype(jnp.int32).astype(jnp.float32))
     highest = functools.reduce(jnp.maximum, peaks)
     bottom, top = 0.0, 0.0
-    for m, l, s in zip(peaks, totals, sums):
+    for m, l, g, s in zip(peaks, totals, scales, sums):
         scale = jnp.exp2(m - highest)
         bottom = bottom + l * scale
-        top = top + s * scale
+        top = top + s * (g * scale)
     result = top / bottom
     for h in range(own):
         for s in range(steps):
             at = h * moments + s * parts
             att_ref[s, :, h * HEAD_DIM : (h + 1) * HEAD_DIM] = result[at : at + parts]
 
+    q_copy(pair, column, r_send.at[column]).wait_send()
+    for i in order:
+        for peer in same_side(i):
+            q_copy(peer, column, q_send.at[peer]).wait_send()
+            q_copy(pair, peer, r_send.at[peer]).wait_send()
     for o in range(1, n_ctx):
         peer = lax.rem(column + o, n_ctx)
-        q_copy(peer, column).wait_send()
-        p_copy(peer, column).wait_send()
+        for copy in p_copies(peer, column):
+            copy.wait_send()
     for delta in FAR:
         @pl.when(inside(delta))
         def _():
             a_copy(delta).wait_send()
-            w_copy(delta).wait_send()
+            for copy in w_copies(delta):
+                copy.wait_send()
 
 
 def solution(mesh):
@@ -303,8 +371,9 @@
         positions = prompt_kv.shape[0]
         own = HEADS // n_ctx
         rows = own * steps * parts
-        cache = jnp.concatenate([suffix_kv, jnp.transpose(new_kv, (1, 0, 2))], axis=1)
-        cache = cache.reshape(parts * slots, width)
+        old = jnp.transpose(suffix_kv, (1, 0, 2)).reshape(history * parts, width)
+        new = new_kv.reshape(steps * parts, width)
+        anywhere = pl.BlockSpec(memory_space=pl.ANY)
         vmem = pl.BlockSpec(memory_space=pltpu.VMEM)
         dma = pltpu.SemaphoreType.DMA
         attended, suffix_out = pl.pallas_call(
@@ -313,30 +382,33 @@
                 jax.ShapeDtypeStruct((steps, parts, own * HEAD_DIM), jnp.float32),
                 jax.ShapeDtypeStruct((parts * slots, width), jnp.bfloat16),
             ),
-            in_specs=[pl.BlockSpec(memory_space=pl.ANY), vmem, vmem, vmem],
+            in_specs=[anywhere] * 5,
             out_specs=(vmem, vmem),
             scratch_shapes=[
                 pltpu.VMEM((key_heads, positions, HEAD_DIM), jnp.bfloat16),
                 pltpu.VMEM((key_heads, positions, HEAD_DIM), jnp.bfloat16),
+                pltpu.VMEM((steps, parts, own * HEAD_DIM), jnp.bfloat16),
+                pltpu.VMEM((steps, parts), jnp.int32),
                 pltpu.VMEM((n_ctx, rows, HEAD_DIM), jnp.bfloat16),
-                pltpu.VMEM((n_ctx, rows + 8, HEAD_DIM), jnp.float32),
-                pltpu.VMEM((n_ctx, rows + 8, HEAD_DIM), jnp.float32),
+                pltpu.VMEM((n_ctx, rows, HEAD_DIM), jnp.int16),
+                pltpu.VMEM((n_ctx, rows, HEAD_DIM), jnp.int16),
+                pltpu.VMEM((n_ctx, 8, LANES), jnp.float32),
+                pltpu.VMEM((n_ctx, 8, LANES), jnp.float32),
                 pltpu.VMEM((2 * SPAN + 1, parts * slots, width), jnp.bfloat16),
                 pltpu.VMEM((2 * SPAN + 1, 8, LANES), jnp.int32),
-                dma((key_heads, 2)),
-                dma((n_ctx,)), dma((n_ctx,)), dma((n_ctx,)), dma((n_ctx,)),
-                dma((2 * SPAN + 1,)), dma((2 * SPAN + 1,)),
-                dma((2 * SPAN + 1,)), dma((2 * SPAN + 1,)),
+                dma((key_heads, 2)), dma((4,)),
+                *[dma((n_ctx,))] * 7,
+                *[dma((2 * SPAN + 1,))] * 6,
             ],
             compiler_params=pltpu.CompilerParams(
-                collective_id=0, has_side_effects=True, vmem_limit_bytes=48 * 1024 * 1024
+                collective_id=0, has_side_effects=True, vmem_limit_bytes=60 * 1024 * 1024
             ),
             cost_estimate=pl.CostEstimate(
                 flops=4 * HEADS * steps * parts * positions * HEAD_DIM,
                 bytes_accessed=4 * positions * width,
                 transcendentals=HEADS * steps * parts * positions,
             ),
-        )(prompt_kv, cache, queries, ancestors)
+        )(prompt_kv, old, new, queries, ancestors)
         return attended, suffix_out.reshape(parts, slots, width)
 
     return jax.shard_map(

time: 32.3 us -> 27.4 us (0.85)
  the two profiles are of different devices: /device:TPU:15 before, /device:TPU:0 now
where the time goes in v2:
time: 27.4 us; the launch traced here: 27.2 us
  Pallas kernels  23.4 us (85%)
  local copies, waits for them, and re-layouts  3.14 us (11%)
  between operations  0.64 us (2%)
    pallas_call x1, Pallas kernels, shards(): pl.pallas_call(functools.partial(kernel, n_ctx, n_dom, key_heads, steps,...  23.4 us
    unnamed x2, local copies, waits for them, and re-layouts  3.14 us

profile of v2, /device:TPU:0, one launch (start us, length us, event | category | flops | bytes accessed | tf_op | source)
XLA Modules:
  0.0 27.2 jit_solution(12306848169255308994)
XLA Ops:
  0.6 23.4 %shard_map.68 = (f32[4,8,512]{2,1,0:T(8,128)}, bf16[128,1024]{1,0:T(8,128)(2,1)}) custom-call(bf16[2048,1024]{1,0:T(8,128)(2,1)} %kv_ref.1, bf16[96,1024]{1,0:T(8,128)(2,1)} %bitcast.6, bf16[32,1024]{1,0:T(8,128)(2,1)} %bitcast.7, bf16[4,8,512]{2,1,0:T(8,128)(2,1)} %q_ref.1, s32[4,8]{1,0:T(4,128)} %anc_ref.1), custom_call_target="tpu_custom_call" | custom-call | flops 1073741824 | bytes 8388608 | tf_op jit(solution)/shard_map/pallas_call | solution.py:379
  24.0 1.5 %copy.9 = f32[4,8,512]{2,1,0:T(8,128)} copy(f32[4,8,512]{2,1,0:T(8,128)} %get-tuple-element.8) | data formatting | bytes 131072
  25.5 1.7 %copy.10 = bf16[8,16,1024]{2,1,0:T(8,128)(2,1)} copy(bf16[8,16,1024]{2,1,0:T(8,128)(2,1)} %bitcast.5) | data formatting | bytes 524288

commit v3 on v2

--- a/solution.py
+++ b/solution.py
@@ -32,7 +32,7 @@
     kv_ref, old_ref, new_ref, q_ref, anc_ref,
     att_ref, out_ref,
     k_buf, v_buf, q_raw, anc_raw, q_all, part, got, part_stats, got_stats, window, anc_win,
-    kv_sem, in_sem, q_send, q_recv, r_send, p_send, p_recv, t_send, t_recv,
+    kv_sem, in_sem, q_send, q_recv, p_send, p_recv, t_send, t_recv,
     w_send, w_recv, n_send, n_recv, a_send, a_recv,
 ):
     column = lax.axis_index("ctx")
@@ -49,7 +49,25 @@
     factor = LOG2E / HEAD_DIM**0.5
 
     pair = column + 1 - 2 * (column % 2)
-    order = [0] + sorted(range(1, key_heads), key=lambda i: (i < key_heads // 2, i))
+    order = [0] + list(range(1, key_heads))
+
+    q_in = pltpu.make_async_copy(q_ref, q_raw, in_sem.at[0])
+    anc_in = pltpu.make_async_copy(anc_ref, anc_raw, in_sem.at[1])
+    q_in.start()
+    anc_in.start()
+    barrier = pltpu.get_barrier_semaphore()
+    for o in range(1, n_ctx):
+        pl.semaphore_signal(
+            barrier, inc=1, device_id={"ctx": lax.rem(column + o, n_ctx)}, device_id_type=MESH
+        )
+
+    def inside(delta):
+        return (row + delta >= 0) & (row + delta < n_dom)
+
+    for delta in FAR:
+        @pl.when(inside(delta))
+        def _():
+            pl.semaphore_signal(barrier, inc=1, device_id={"dom": row + delta}, device_id_type=MESH)
 
     def head_at(i):
         e, bit = my_head, 1
@@ -78,34 +96,16 @@
             ),
         )
 
-    q_in = pltpu.make_async_copy(q_ref, q_raw, in_sem.at[0])
-    anc_in = pltpu.make_async_copy(anc_ref, anc_raw, in_sem.at[1])
     old_rows, new_rows = old_ref.shape[0], new_ref.shape[0]
     old_in = pltpu.make_async_copy(old_ref, window.at[SPAN, pl.ds(0, old_rows)], in_sem.at[2])
     new_in = pltpu.make_async_copy(
         new_ref, window.at[SPAN, pl.ds(old_rows, new_rows)], in_sem.at[3]
     )
-    q_in.start()
-    anc_in.start()
     for i in order:
         for copy in loads(i):
             copy.start()
     old_in.start()
     new_in.start()
-
-    barrier = pltpu.get_barrier_semaphore()
-    for o in range(1, n_ctx):
-        pl.semaphore_signal(
-            barrier, inc=1, device_id={"ctx": lax.rem(column + o, n_ctx)}, device_id_type=MESH
-        )
-
-    def inside(delta):
-        return (row + delta >= 0) & (row + delta < n_dom)
-
-    for delta in FAR:
-        @pl.when(inside(delta))
-        def _():
-            pl.semaphore_signal(barrier, inc=1, device_id={"dom": row + delta}, device_id_type=MESH)
 
     q_in.wait()
     anc_in.wait()
@@ -136,15 +136,18 @@
             device_id={"ctx": peer}, device_id_type=MESH,
         )
 
-    def relay(i):
+    def other(peer):
+        return peer + 1 - 2 * (peer % 2)
+
+    def arrive(i):
         for source in same_side(i):
             q_copy(source, source, q_send.at[source]).wait_recv()
-            q_copy(pair, source, r_send.at[source]).start()
-
-    q_copy(pair, column, r_send.at[column]).start()
+
+    q_copy(pair, column, q_send.at[pair]).start()
     for i in order:
         for peer in same_side(i):
             q_copy(peer, column, q_send.at[peer]).start()
+            q_copy(other(peer), column, q_send.at[other(peer)]).start()
 
     def w_pieces(delta, at, sent, landed):
         return [
@@ -208,12 +211,11 @@
             turned = jnp.concatenate([turned, jnp.zeros((8, LANES - n), jnp.float32)], axis=1)
         return turned
 
-    relay(0)
-    relay(order[1])
     for n, i in enumerate(order):
         e = head_at(i)
         for copy in loads(i):
             copy.wait()
+        arrive(i)
         for o in range(members // 2):
             source = e * members + 2 * o + pair % 2
             q_copy(source, source, q_send.at[source]).wait_recv()
@@ -239,9 +241,6 @@
             else:
                 for copy in p_copies(peer, column):
                     copy.start()
-        if n == 0:
-            for later in order[2:]:
-                relay(later)
 
     for delta in FAR:
         @pl.when(inside(delta))
@@ -250,11 +249,11 @@
     known = anc_win[0]
     for w in range(1, 2 * SPAN + 1):
         known = jnp.maximum(known, anc_win[w])
-    known = jnp.where(known >= 0, lax.rem(known, LANES), -1)
+    known = jnp.where(known >= 0, known & (LANES - 1), -1)
     q_id = lax.broadcasted_iota(jnp.int32, (LANES, LANES), 0)
-    one = lax.broadcasted_iota(jnp.int32, (parts, LANES), 1) == lax.rem(
-        row * parts + lax.broadcasted_iota(jnp.int32, (parts, LANES), 0), LANES
-    )
+    one = lax.broadcasted_iota(jnp.int32, (parts, LANES), 1) == (
+        row * parts + lax.broadcasted_iota(jnp.int32, (parts, LANES), 0)
+    ) & (LANES - 1)
     one = one.astype(jnp.float32)
     zero = jnp.zeros_like(one)
     origin = {}
@@ -272,15 +271,14 @@
     ).astype(jnp.bfloat16)
     cols = (2 * SPAN + 1) * parts * slots
     block = (steps + 1) * parts
-    col = lax.broadcasted_iota(jnp.int32, (LANES, cols), 1)
-    particle = lax.rem(
-        (row - SPAN + col // (parts * slots)) * parts + col % parts + 16 * LANES, LANES
-    )
+    p_bits, s_bits = parts.bit_length() - 1, slots.bit_length() - 1
+    col = lax.broadcasted_iota(jnp.int32, (1, cols), 1)
+    particle = ((row - SPAN + (col >> (p_bits + s_bits))) * parts + (col & (parts - 1))) & (LANES - 1)
+    slot = (col >> p_bits) & (slots - 1)
     spread = (particle == lax.broadcasted_iota(jnp.int32, (LANES, cols), 0)).astype(
         jnp.float32
     ).astype(jnp.bfloat16)
     from_where = nn(stack, spread)
-    slot = lax.broadcasted_iota(jnp.int32, (block, cols), 1) // parts % slots
     kind = jnp.maximum(slot - history, 0)
     valid = jnp.zeros((block, cols), jnp.float32)
     for k in range(steps):
@@ -295,9 +293,7 @@
     new_in.wait()
 
     pick = jnp.broadcast_to(valid[moments:, None, :], (parts, slots, cols)).reshape(parts * slots, cols)
-    same = lax.broadcasted_iota(jnp.int32, (parts * slots, cols), 1) // parts % slots == lax.rem(
-        lax.broadcasted_iota(jnp.int32, (parts * slots, cols), 0), slots
-    )
+    same = slot == lax.broadcasted_iota(jnp.int32, (parts * slots, 1), 0) & (slots - 1)
     pick = jnp.where(same, pick, 0.0).astype(jnp.bfloat16)
     for c in range(0, 2 * key_width, 256):
         piece = window[:, :, c : c + 256].reshape(cols, 256)
@@ -319,18 +315,21 @@
         source = lax.rem(column + o, n_ctx)
         for copy in p_copies(source, source):
             copy.wait_recv()
+    sources = [lax.rem(column + o, n_ctx) for o in range(n_ctx)]
     peaks, totals, scales, sums = [peak], [total], [1.0], [summed]
-    for o in range(n_ctx):
-        source = lax.rem(column + o, n_ctx)
-        codes = part[column] if o == 0 else got[source]
-        tile = part_stats[column] if o == 0 else got_stats[source]
-        stats = jnp.transpose(
-            jnp.concatenate([tile, jnp.zeros((LANES - 8, LANES), jnp.float32)], axis=0)
-        )[:rows]
-        peaks.append(stats[:, 0:1])
-        totals.append(stats[:, 1:2])
-        scales.append(stats[:, 2:3] * (1.0 / CODES))
-        sums.append(codes.astype(jnp.int32).astype(jnp.float32))
+    group = LANES // 8
+    for first in range(0, n_ctx, group):
+        some = range(first, min(first + group, n_ctx))
+        tiles = [part_stats[column] if o == 0 else got_stats[sources[o]] for o in some]
+        if len(tiles) < group:
+            tiles.append(jnp.zeros((LANES - 8 * len(tiles), LANES), jnp.float32))
+        stats = jnp.transpose(jnp.concatenate(tiles, axis=0))[:rows]
+        for n, o in enumerate(some):
+            codes = part[column] if o == 0 else got[sources[o]]
+            peaks.append(stats[:, 8 * n : 8 * n + 1])
+            totals.append(stats[:, 8 * n + 1 : 8 * n + 2])
+            scales.append(stats[:, 8 * n + 2 : 8 * n + 3] * (1.0 / CODES))
+            sums.append(codes.astype(jnp.int32).astype(jnp.float32))
     highest = functools.reduce(jnp.maximum, peaks)
     bottom, top = 0.0, 0.0
     for m, l, g, s in zip(peaks, totals, scales, sums):
@@ -343,11 +342,11 @@
             at = h * moments + s * parts
             att_ref[s, :, h * HEAD_DIM : (h + 1) * HEAD_DIM] = result[at : at + parts]
 
-    q_copy(pair, column, r_send.at[column]).wait_send()
+    q_copy(pair, column, q_send.at[pair]).wait_send()
     for i in order:
         for peer in same_side(i):
             q_copy(peer, column, q_send.at[peer]).wait_send()
-            q_copy(pair, peer, r_send.at[peer]).wait_send()
+            q_copy(other(peer), column, q_send.at[other(peer)]).wait_send()
     for o in range(1, n_ctx):
         peer = lax.rem(column + o, n_ctx)
         for copy in p_copies(peer, column):
@@ -373,7 +372,7 @@
         rows = own * steps * parts
         old = jnp.transpose(suffix_kv, (1, 0, 2)).reshape(history * parts, width)
         new = new_kv.reshape(steps * parts, width)
-        anywhere = pl.BlockSpec(memory_space=pl.ANY)
+        hbm = pl.BlockSpec(memory_space=pltpu.HBM)
         vmem = pl.BlockSpec(memory_space=pltpu.VMEM)
         dma = pltpu.SemaphoreType.DMA
         attended, suffix_out = pl.pallas_call(
@@ -382,7 +381,7 @@
                 jax.ShapeDtypeStruct((steps, parts, own * HEAD_DIM), jnp.float32),
                 jax.ShapeDtypeStruct((parts * slots, width), jnp.bfloat16),
             ),
-            in_specs=[anywhere] * 5,
+            in_specs=[hbm] * 5,
             out_specs=(vmem, vmem),
             scratch_shapes=[
                 pltpu.VMEM((key_heads, positions, HEAD_DIM), jnp.bfloat16),
@@ -397,7 +396,7 @@
                 pltpu.VMEM((2 * SPAN + 1, parts * slots, width), jnp.bfloat16),
                 pltpu.VMEM((2 * SPAN + 1, 8, LANES), jnp.int32),
                 dma((key_heads, 2)), dma((4,)),
-                *[dma((n_ctx,))] * 7,
+                *[dma((n_ctx,))] * 6,
                 *[dma((2 * SPAN + 1,))] * 6,
             ],
             compiler_params=pltpu.CompilerParams(

time: 27.4 us -> 26.5 us (0.967)
  Pallas kernels: 23.4 us -> 22.5 us
    pallas_call x1, Pallas kernels: 23.4 us -> 22.5 us  [shards(): pl.pallas_call(functools.partial(kernel, n_ctx, n_dom, key_heads, steps,...]
where the time goes in v3:
time: 26.5 us; the launch traced here: 26.3 us
  Pallas kernels  22.5 us (85%)
  local copies, waits for them, and re-layouts  3.14 us (12%)
  between operations  0.64 us (2%)
    pallas_call x1, Pallas kernels, shards(): pl.pallas_call(functools.partial(kernel, n_ctx, n_dom, key_heads, steps,...  22.5 us
    unnamed x2, local copies, waits for them, and re-layouts  3.14 us

profile of v3, /device:TPU:0, one launch (start us, length us, event | category | flops | bytes accessed | tf_op | source)
XLA Modules:
  0.0 26.3 jit_solution(9059841397145372638)
XLA Ops:
  0.6 22.5 %shard_map.68 = (f32[4,8,512]{2,1,0:T(8,128)}, bf16[128,1024]{1,0:T(8,128)(2,1)}) custom-call(bf16[2048,1024]{1,0:T(8,128)(2,1)} %kv_ref.1, bf16[96,1024]{1,0:T(8,128)(2,1)} %bitcast.6, bf16[32,1024]{1,0:T(8,128)(2,1)} %bitcast.7, bf16[4,8,512]{2,1,0:T(8,128)(2,1)} %q_ref.1, s32[4,8]{1,0:T(4,128)} %anc_ref.1), custom_call_target="tpu_custom_call" | custom-call | flops 1073741824 | bytes 8388608 | tf_op jit(solution)/shard_map/pallas_call | solution.py:378
  23.2 1.5 %copy.9 = f32[4,8,512]{2,1,0:T(8,128)} copy(f32[4,8,512]{2,1,0:T(8,128)} %get-tuple-element.8) | data formatting | bytes 131072
  24.7 1.7 %copy.10 = bf16[8,16,1024]{2,1,0:T(8,128)(2,1)} copy(bf16[8,16,1024]{2,1,0:T(8,128)(2,1)} %bitcast.5) | data formatting | bytes 524288

commit v4 on v3

--- a/solution.py
+++ b/solution.py
@@ -30,8 +30,8 @@
 def kernel(
     n_ctx, n_dom, key_heads, steps, history,
     kv_ref, old_ref, new_ref, q_ref, anc_ref,
-    att_ref, out_ref,
-    k_buf, v_buf, q_raw, anc_raw, q_all, part, got, part_stats, got_stats, window, anc_win,
+    att_ref, suffix_out,
+    k_buf, v_buf, q_raw, anc_raw, q_all, part, got, part_stats, got_stats, window, anc_win, out_ref,
     kv_sem, in_sem, q_send, q_recv, p_send, p_recv, t_send, t_recv,
     w_send, w_recv, n_send, n_recv, a_send, a_recv,
 ):
@@ -299,6 +299,9 @@
         piece = window[:, :, c : c + 256].reshape(cols, 256)
         out_ref[:, c : c + 256] = nn(pick, piece).astype(jnp.bfloat16)
 
+    suffix_write = pltpu.make_async_copy(out_ref, suffix_out, in_sem.at[4])
+    suffix_write.start()
+
     at = pl.multiple_of(my_head * HEAD_DIM, HEAD_DIM)
     keys = window[:, :, pl.ds(at, HEAD_DIM)].reshape(cols, HEAD_DIM)
     vals = window[:, :, pl.ds(pl.multiple_of(at + key_width, HEAD_DIM), HEAD_DIM)].reshape(
@@ -357,6 +360,7 @@
             a_copy(delta).wait_send()
             for copy in w_copies(delta):
                 copy.wait_send()
+    suffix_write.wait()
 
 
 def solution(mesh):
@@ -382,7 +386,7 @@
                 jax.ShapeDtypeStruct((parts * slots, width), jnp.bfloat16),
             ),
             in_specs=[hbm] * 5,
-            out_specs=(vmem, vmem),
+            out_specs=(vmem, hbm),
             scratch_shapes=[
                 pltpu.VMEM((key_heads, positions, HEAD_DIM), jnp.bfloat16),
                 pltpu.VMEM((key_heads, positions, HEAD_DIM), jnp.bfloat16),
@@ -395,7 +399,8 @@
                 pltpu.VMEM((n_ctx, 8, LANES), jnp.float32),
                 pltpu.VMEM((2 * SPAN + 1, parts * slots, width), jnp.bfloat16),
                 pltpu.VMEM((2 * SPAN + 1, 8, LANES), jnp.int32),
-                dma((key_heads, 2)), dma((4,)),
+                pltpu.VMEM((parts * slots, width), jnp.bfloat16),
+                dma((key_heads, 2)), dma((5,)),
                 *[dma((n_ctx,))] * 6,
                 *[dma((2 * SPAN + 1,))] * 6,
             ],

time: 26.5 us -> 26.4 us (level)
  no operation moved by 1% of the time
where the time goes in v4:
time: 26.4 us; the launch traced here: 26.2 us
  Pallas kernels  22.5 us (85%)
  local copies, waits for them, and re-layouts  3.14 us (12%)
  between operations  0.64 us (2%)
    pallas_call x1, Pallas kernels, shards(): pl.pallas_call(functools.partial(kernel, n_ctx, n_dom, key_heads, steps,...  22.5 us
    unnamed x2, local copies, waits for them, and re-layouts  3.14 us

profile of v4, /device:TPU:0, one launch (start us, length us, event | category | flops | bytes accessed | tf_op | source)
XLA Modules:
  0.0 26.2 jit_solution(14370303013816629310)
XLA Ops:
  0.6 22.5 %shard_map.68 = (f32[4,8,512]{2,1,0:T(8,128)}, bf16[128,1024]{1,0:T(8,128)(2,1)}) custom-call(bf16[2048,1024]{1,0:T(8,128)(2,1)} %kv_ref.1, bf16[96,1024]{1,0:T(8,128)(2,1)} %bitcast.6, bf16[32,1024]{1,0:T(8,128)(2,1)} %bitcast.7, bf16[4,8,512]{2,1,0:T(8,128)(2,1)} %q_ref.1, s32[4,8]{1,0:T(4,128)} %anc_ref.1), custom_call_target="tpu_custom_call" | custom-call | flops 1073741824 | bytes 8388608 | tf_op jit(solution)/shard_map/pallas_call | solution.py:382
  23.1 1.5 %copy.9 = f32[4,8,512]{2,1,0:T(8,128)} copy(f32[4,8,512]{2,1,0:T(8,128)} %get-tuple-element.8) | data formatting | bytes 131072
  24.6 1.7 %copy.10 = bf16[8,16,1024]{2,1,0:T(8,128)(2,1)} copy(bf16[8,16,1024]{2,1,0:T(8,128)(2,1)} %bitcast.5) | data formatting | bytes 524288
